TPU v7x, 512 devices: a whole 4x4x16 slice. The times are simulated.
512 devices in a mesh: dp: 128 (over y, z, core), tensor: 4 (over x).
Axes of the slice: x: 4, y: 4, z: 16, core: 2. Of those that a mesh axis runs over, the one named last changes fastest.
Arguments:
- tokens: bfloat16 [32768, 4096], P('dp', 'tensor'), may hold values from -6 to 6
- out_grad: bfloat16 [32768, 14336], P('dp', 'tensor'), may hold values from -6 to 6
- proj_in: bfloat16 [4096, 64], P('tensor'), may hold values from -0.09375 to 0.09375
- proj_out: bfloat16 [14336, 64], P('tensor'), may hold values from -0.046875 to 0.046875
- source_ids: int32 [512], P('dp'), may hold values from 0 to 255, as said below
- slot_of_source: int32 [256], replicated, may hold values from 0 to 255, as said below
Outputs:
- source_sketch: float32 [256, 4096], P('dp', 'tensor')
Inputs may be any that keep to these rules, and one draw needn't show every extreme that they name: `source_ids`: sequences j * 4, j * 4 + 1 and j * 4 + 2 belong to sources whose output rows lie in the blocks of 2 rows numbered j - 1, j + 1 and j + 64, counted round; the other sequences' sources follow a skewed law. `slot_of_source`: each output row is named by exactly one source.
All inputs are finite; a program needn't handle non-finite values.
Results may differ from a plain program's by a relative error of at most 0.0003.
Values sent between devices are 32-bit elements; how exact they have to be, the bound alone decides.
A program may use at most 64 MiB of HBM per device.

v0:
```python
import jax
import jax.numpy as jnp
from jax import lax
from jax.sharding import PartitionSpec as P


def local(tokens, out_grad, proj_in, proj_out, source_ids, slot_of_source):
    width = proj_in.shape[1]
    groups = lax.axis_size("tensor")
    my_rows = width // groups
    member = lax.axis_index("tensor")
    xp_part = jnp.dot(tokens, proj_in, preferred_element_type=jnp.float32)
    gp_part = jnp.dot(out_grad, proj_out, preferred_element_type=jnp.float32)
    xp, gp = lax.psum((xp_part, gp_part), "tensor")
    gp_mine = lax.dynamic_slice_in_dim(gp, member * my_rows, my_rows, 1)
    count = source_ids.shape[0]
    length = tokens.shape[0] // count
    xs = xp.reshape(count, length, width)
    gs = gp_mine.reshape(count, length, my_rows)
    sketch = jnp.einsum("sla,slb->sab", gs, xs, precision=lax.Precision.HIGHEST) * length ** (-0.5)
    sketch = sketch.reshape(count, my_rows * width)
    total_sources = slot_of_source.shape[0]
    source_range = jnp.arange(total_sources, dtype=jnp.int32)
    slots = jnp.sum(
        jnp.where(source_ids[:, None] == source_range[None, :], slot_of_source[None, :], 0), axis=1
    )
    owned_count = total_sources // lax.axis_size("dp")
    wanted = jnp.arange(owned_count * lax.axis_size("dp"), dtype=jnp.int32)
    select = (wanted[:, None] == slots[None, :]).astype(jnp.float32)
    return lax.psum_scatter(
        jnp.dot(select, sketch, precision=lax.Precision.HIGHEST),
        "dp",
        scatter_dimension=0,
        tiled=True,
    )


def solution(mesh):
    placed = (
        P("dp", "tensor"),
        P("dp", "tensor"),
        P("tensor", None),
        P("tensor", None),
        P("dp"),
        P(),
    )
    return jax.shard_map(
        local, mesh=mesh, in_specs=placed, out_specs=P("dp", "tensor"), check_vma=False
    )
```

profile of v0, /device:TPU:1, one launch (start us, length us, event | category | flops | bytes accessed | tf_op | source)
XLA Modules:
  0.0 420.6 jit_solution(3711370981554200536)
XLA Ops:
  6.5 0.0 copy-start
  6.5 0.0 copy-start.2
  6.5 0.0 copy-start.1
  6.5 0.0 all-reduce.7.cloned.1.call-start
  6.5 2.1 fusion.4
  8.7 0.0 copy-done
  8.7 2.3 fusion.3
  11.0 0.0 all-reduce.7.cloned.1.call-update
  11.0 0.0 all-reduce.5.cloned.1.call-start
  11.1 0.0 copy-done.2
  11.1 0.0 copy-done.1
  11.1 0.2 select_reduce_fusion
  11.3 60.0 %all-reduce.7.cloned.1.call-done = (f32[4,64,64]{2,1,0:T(8,128)}, f32[256,64]{0,1:T(8,128)}) async-done(((f32[4,64,64]{2,1,0:T(8,128)}, f32[256,64]{0,1:T(8,128)}), (f32[4,64,64]{2,1,0:T(8,128)}, f32[256,64]{0,1:T(8,128)})) %all-reduce.7.cloned.1.call-update) | async-done | bytes 131088 | tf_op jit(solution)/shard_map/psum | solution.py:14
  71.3 0.7 constant_dynamic-slice_fusion.1
  72.0 0.1 reshape.12
  72.1 1.1 convolution_multiply_fusion
  73.2 0.1 reshape.14
  73.3 1.6 fusion
  74.9 0.0 all-reduce.5.cloned.1.call-update
  74.9 1.3 dynamic-slice
  76.8 335.6 %all-reduce.5.cloned.1.call-done = f32[256,1024]{1,0:T(8,128)} async-done(((f32[256,1024]{1,0:T(8,128)}), f32[256,1024]{1,0:T(8,128)}) %all-reduce.5.cloned.1.call-update) | async-done | bytes 1048592
  412.4 1.4 constant_dynamic-slice_fusion
Async XLA Ops:
  6.5 2.1 copy-start
  6.5 4.5 %copy-start.2 = (s32[4]{0:T(128)S(1)}, s32[4]{0:T(128)}, u32[]{:S(2)}) copy-start(s32[4]{0:T(128)} %param.10) | copy-start | bytes 52
  6.5 4.5 %copy-start.1 = (s32[256]{0:T(256)S(1)}, s32[256]{0:T(256)}, u32[]{:S(2)}) copy-start(s32[256]{0:T(256)} %param.11) | copy-start | bytes 3076
  6.5 64.7 %all-reduce.7.cloned.1.call-start = ((), (), s32[]{:S(2)}) async-start(), calls=%async_computation.1 | async-start | bytes 393216 | tf_op jit(solution)/shard_map/psum | solution.py:14
  11.0 401.4 %all-reduce.5.cloned.1.call-start = ((), (), s32[]{:S(2)}) async-start(), calls=%async_computation | async-start | bytes 2097152
Sparse Core Ops, SparseCore 0:
  11.1 60.0 all-reduce.6
  75.1 337.2 all-reduce.4
where the time goes:
time: 421 us
  waiting for transfers between devices  396 us (94%)
  between operations  14.1 us (3%)
  matrix products  7.14 us (2%)
    unnamed x3, waiting for transfers between devices  336 us
    psum x1, waiting for transfers between devices, local(): xp, gp = lax.psum((xp_part, gp_part), 'tensor')  60 us
  transfers between devices with their start and end apart: 2, of which 2 were waited for; matrix products, arithmetic and copies ran while one was open for 0% of the time, Pallas kernels for 0%

commit v1 on v0

v1 whole, which is shorter than its diff:
```python
import functools

import jax
import jax.numpy as jnp
from jax import lax
from jax.experimental import pallas as pl
from jax.experimental.pallas import tpu as pltpu
from jax.sharding import PartitionSpec as P

MESH = pl.DeviceIdType.MESH
F32 = jnp.float32
CORES = 2
COLUMNS = 4


def project(rows, weights):
    return lax.dot_general(rows, weights, (((1,), (1,)), ((), ())), preferred_element_type=F32)


def kernel(
    ny, nz, nx, length,
    tok_hbm, og_hbm, pin_hbm, pout_hbm, src_hbm, slot_hbm,
    out_ref,
    tok, og, pin, pout, src, slot_of,
    mine_last, mine_rest, recv_last, recv_rest, gram,
    held, ids, fixed_out, fixed_in, spread_out, spread_in,
    load_sem, xl_send, xl_recv, xr_send, xr_recv,
    id_send, id_recv, gather_send, gather_recv,
    fixed_send, fixed_recv, spread_send, spread_recv,
):
    j = lax.axis_index("dp")
    m = lax.axis_index("tensor")
    ndp = ny * nz * CORES
    half = ndp // 2
    core = lax.rem(j, CORES)
    z = lax.rem(lax.div(j, CORES), nz)
    y = lax.div(j, CORES * nz)
    rest = 3 * length
    quarter = 64 // nx

    def dp_of(yy, zz, cc):
        return (yy * nz + zz) * CORES + cc

    loads = [
        (src_hbm, src),
        (slot_hbm, slot_of),
        (pout_hbm, pout),
        (og_hbm.at[pl.ds(rest, length)], og.at[pl.ds(rest, length)]),
        (pin_hbm, pin),
        (tok_hbm.at[pl.ds(rest, length)], tok.at[pl.ds(rest, length)]),
        (og_hbm.at[pl.ds(0, rest)], og.at[pl.ds(0, rest)]),
        (tok_hbm.at[pl.ds(0, rest)], tok.at[pl.ds(0, rest)]),
    ]
    loads = [pltpu.make_async_copy(a, b, load_sem.at[i]) for i, (a, b) in enumerate(loads)]
    for load in loads:
        load.start()

    barrier = pltpu.get_barrier_semaphore()
    x_peers = [(j, lax.rem(m + d, nx)) for d in range(1, nx)]
    z_peers = [(dp_of(y, lax.rem(z + d, nz), core), m) for d in range(1, nz)]
    spread = [(dy, dc) for dy in range(ny) for dc in range(CORES)]
    spread_peers = [
        (dp_of(lax.rem(y + dy, ny), z, lax.rem(core + dc, CORES)), m) for dy, dc in spread
    ]
    fixed_to = [lax.rem(j + ndp - 1, ndp), lax.rem(j + 1, ndp), lax.rem(j + half, ndp)]
    fixed_peers = [(t, m) for t in fixed_to]
    greeted = x_peers + z_peers + spread_peers[1:] + fixed_peers
    for peer in greeted:
        pl.semaphore_signal(barrier, inc=1, device_id=peer, device_id_type=MESH)

    loads[0].wait()
    loads[1].wait()
    slots = [slot_of[src[i]] for i in range(4)]
    ids[0] = jnp.full((1, 128), slots[3], jnp.int32)

    for i in (2, 3, 4, 5):
        loads[i].wait()
    xp = project(tok[pl.ds(rest, length), :], pin[...])
    gp = project(og[pl.ds(rest, length), :], pout[...])
    mine_last[...] = jnp.concatenate([xp, gp], axis=1)

    pl.semaphore_wait(barrier, len(greeted))
    for d in range(1, nx):
        pltpu.make_async_remote_copy(
            mine_last, recv_last.at[nx - 1 - d], xl_send, xl_recv,
            device_id=x_peers[d - 1], device_id_type=MESH,
        ).start()
    for d in range(1, nz):
        pltpu.make_async_remote_copy(
            ids.at[0], ids.at[nz - d], id_send, id_recv,
            device_id=z_peers[d - 1], device_id_type=MESH,
        ).start()

    loads[6].wait()
    loads[7].wait()
    xp = project(tok[pl.ds(0, rest), :], pin[...])
    gp = project(og[pl.ds(0, rest), :], pout[...])
    mine_rest[...] = jnp.concatenate([xp, gp], axis=1)
    for d in range(1, nx):
        pltpu.make_async_remote_copy(
            mine_rest, recv_rest.at[nx - 1 - d], xr_send, xr_recv,
            device_id=x_peers[d - 1], device_id_type=MESH,
        ).start()

    lane = lax.broadcasted_iota(jnp.int32, (8, 128), 1)

    def sketch(total, at):
        gram[at] = lax.dot_general(
            total, total, (((0,), (0,)), ((), ())),
            precision=lax.Precision.HIGHEST, preferred_element_type=F32,
        ) * (length ** -0.5)
        start = 64 + m * quarter
        even = gram[at, pl.ds(start, quarter // 2, stride=2), :]
        odd = gram[at, pl.ds(start + 1, quarter // 2, stride=2), :]
        return jnp.where(lane < 64, even, pltpu.roll(odd, 64, 1))

    pltpu.make_async_copy(recv_last, recv_last, xl_recv).wait()
    total = mine_last[...]
    for d in range(nx - 1):
        total = total + recv_last[d]
    held[0] = sketch(total, 0)
    for d in range(1, nz):
        pltpu.make_async_remote_copy(
            held.at[0], held.at[nz - d], gather_send, gather_recv,
            device_id=z_peers[d - 1], device_id_type=MESH,
        ).start()

    pltpu.make_async_copy(recv_rest, recv_rest, xr_recv).wait()
    for s in range(3):
        rows = pl.ds(s * length, length)
        total = mine_rest[rows, :]
        for d in range(nx - 1):
            total = total + recv_rest[d, rows, :]
        value = sketch(total, 1 + s)
        for w in range(2):
            weight = jnp.where(slots[s] == fixed_to[s] * 2 + w, 1.0, 0.0).astype(F32)
            fixed_out[s, w] = value * weight
        pltpu.make_async_remote_copy(
            fixed_out.at[s], fixed_in.at[s], fixed_send.at[s], fixed_recv.at[s],
            device_id=fixed_peers[s], device_id_type=MESH,
        ).start()

    pltpu.make_async_copy(ids.at[pl.ds(1, nz - 1)], ids.at[pl.ds(1, nz - 1)], id_recv).wait()
    pltpu.make_async_copy(held.at[pl.ds(1, nz - 1)], held.at[pl.ds(1, nz - 1)], gather_recv).wait()
    for t in list(range(1, len(spread))) + [0]:
        dy, dc = spread[t]
        base = spread_peers[t][0] * 2
        for w in range(2):
            acc = jnp.zeros((8, 128), F32)
            for i in range(nz):
                acc = acc + jnp.where(ids[i] == base + w, held[i], 0.0)
            spread_out[t, w] = acc
        if t:
            back = ((ny - dy) % ny) * CORES + dc
            pltpu.make_async_remote_copy(
                spread_out.at[t], spread_in.at[back], spread_send, spread_recv,
                device_id=spread_peers[t], device_id_type=MESH,
            ).start()

    for s in range(3):
        pltpu.make_async_copy(fixed_in.at[s], fixed_in.at[s], fixed_recv.at[s]).wait()
    landed = spread_in.at[pl.ds(1, len(spread) - 1)]
    pltpu.make_async_copy(landed, landed, spread_recv).wait()
    for w in range(2):
        acc = spread_out[0, w]
        for s in range(3):
            acc = acc + fixed_in[s, w]
        for t in range(1, len(spread)):
            acc = acc + spread_in[t, w]
        out_ref[w] = acc

    pltpu.make_async_copy(recv_last, recv_last, xl_send).wait()
    pltpu.make_async_copy(recv_rest, recv_rest, xr_send).wait()
    pltpu.make_async_copy(ids.at[pl.ds(1, nz - 1)], ids.at[pl.ds(1, nz - 1)], id_send).wait()
    pltpu.make_async_copy(held.at[pl.ds(1, nz - 1)], held.at[pl.ds(1, nz - 1)], gather_send).wait()
    for s in range(3):
        pltpu.make_async_copy(fixed_out.at[s], fixed_out.at[s], fixed_send.at[s]).wait()
    pltpu.make_async_copy(landed, landed, spread_send).wait()


def local(ny, nz, nx, tokens, out_grad, proj_in, proj_out, source_ids, slot_of_source):
    length = tokens.shape[0] // source_ids.shape[0]
    width = 2 * proj_in.shape[1]
    pin, pout = proj_in.T, proj_out.T
    spread = ny * CORES
    dma = pltpu.SemaphoreType.DMA
    out = pl.pallas_call(
        functools.partial(kernel, ny, nz, nx, length),
        out_shape=jax.ShapeDtypeStruct((2, 8, 128), F32),
        in_specs=[pl.BlockSpec(memory_space=pltpu.HBM)] * 6,
        out_specs=pl.BlockSpec(memory_space=pltpu.VMEM),
        scratch_shapes=[
            pltpu.VMEM(tokens.shape, tokens.dtype),
            pltpu.VMEM(out_grad.shape, out_grad.dtype),
            pltpu.VMEM(pin.shape, pin.dtype),
            pltpu.VMEM(pout.shape, pout.dtype),
            pltpu.SMEM(source_ids.shape, jnp.int32),
            pltpu.SMEM(slot_of_source.shape, jnp.int32),
            pltpu.VMEM((length, width), F32),
            pltpu.VMEM((3 * length, width), F32),
            pltpu.VMEM((nx - 1, length, width), F32),
            pltpu.VMEM((nx - 1, 3 * length, width), F32),
            pltpu.VMEM((4, width, width), F32),
            pltpu.VMEM((nz, 8, 128), F32),
            pltpu.VMEM((nz, 1, 128), jnp.int32),
            pltpu.VMEM((3, 2, 8, 128), F32),
            pltpu.VMEM((3, 2, 8, 128), F32),
            pltpu.VMEM((spread, 2, 8, 128), F32),
            pltpu.VMEM((spread, 2, 8, 128), F32),
            dma((8,)), dma, dma, dma, dma, dma, dma, dma, dma, dma((3,)), dma((3,)), dma, dma,
        ],
        compiler_params=pltpu.CompilerParams(
            collective_id=0, has_side_effects=True, vmem_limit_bytes=60 * 2**20
        ),
    )(tokens, out_grad, pin, pout, source_ids, slot_of_source)
    return out.reshape(2, 8 * 128)


def solution(mesh):
    nx, ndp = mesh.shape["tensor"], mesh.shape["dp"]
    ny = COLUMNS
    nz = ndp // (ny * CORES)
    placed = (
        P("dp", "tensor"),
        P("dp", "tensor"),
        P("tensor", None),
        P("tensor", None),
        P("dp"),
        P(),
    )
    return jax.shard_map(
        functools.partial(local, ny, nz, nx),
        mesh=mesh, in_specs=placed, out_specs=P("dp", "tensor"), check_vma=False,
    )
```

time: 421 us -> 35.4 us (0.08)
  waiting for transfers between devices: 396 us -> 0 us
  Pallas kernels: 0 us -> 33.9 us
  between operations: 14.1 us -> 0.01 us
  matrix products: 7.14 us -> 0 us
    unnamed x3 -> x0, waiting for transfers between devices: 336 us -> none
    psum x1 -> x0, waiting for transfers between devices: 60 us -> none  [local(): xp, gp = lax.psum((xp_part, gp_part), 'tensor')]
    pallas_call x0 -> x1, Pallas kernels: none -> 33.9 us  [local(): pl.pallas_call(functools.partial(kernel, ny, nz, nx, length), out_shape=j...]
    dot_general x3 -> x0, matrix products: 5.02 us -> none  [the longest x1 2.31 us: local(): gp_part = jnp.dot(out_grad, proj_out, preferred_element_type=jnp.float32)]
  transfers between devices with their start and end apart: 2 -> 0, of which waited for: 2 -> 0; matrix products, arithmetic and copies ran while one was open for 0% -> 0% of each run, Pallas kernels for 0% -> 0%
where the time goes in v1:
time: 35.4 us; the launch traced here: 35.2 us
  Pallas kernels  33.9 us (96%)
  local copies, waits for them, and re-layouts  1.3 us (4%)
    pallas_call x1, Pallas kernels, local(): pl.pallas_call(functools.partial(kernel, ny, nz, nx, length), out_shape=j...  33.9 us
    unnamed x1, local copies, waits for them, and re-layouts  1.3 us

profile of v1, /device:TPU:1, one launch (start us, length us, event | category | flops | bytes accessed | tf_op | source)
XLA Modules:
  0.0 35.2 jit_solution(18416210303531298997)
XLA Ops:
  0.0 33.9 %shard_map.64 = f32[2,8,128]{2,1,0:T(8,128)} custom-call(bf16[256,1024]{1,0:T(8,128)(2,1)} %tok_hbm.1, bf16[256,3584]{1,0:T(8,128)(2,1)} %og_hbm.1, bf16[64,1024]{1,0:T(8,128)(2,1)} %bitcast.7, bf16[64,3584]{1,0:T(8,128)(2,1)} %bitcast.6, s32[4]{0:T(128)} %src_hbm.1, s32[256]{0:T(256)} %slot_hbm.1), custom_call_target="tpu_custom_call" | custom-call | tf_op jit(solution)/shard_map/pallas_call | solution.py:187
  33.9 1.3 %copy.9 = f32[1,2,8,128]{3,1,2,0:T(2,128)} copy(f32[1,2,8,128]{3,2,1,0:T(8,128)} %bitcast.8) | data formatting | bytes 16384

commit v2 on v1

v2 whole, which is shorter than its diff:
```python
import functools

import jax
import jax.numpy as jnp
from jax import lax
from jax.experimental import pallas as pl
from jax.experimental.pallas import tpu as pltpu
from jax.sharding import PartitionSpec as P

MESH = pl.DeviceIdType.MESH
F32 = jnp.float32
CORES = 2
COLUMNS = 4
PACKED = 40


def product(a, b):
    return lax.dot_general(a, b, (((1,), (1,)), ((), ())), preferred_element_type=F32)


def kernel(
    ny, nz, nx, length,
    tok_hbm, og_hbm, pin_hbm, pout_hbm, src_hbm, slot_hbm,
    out_ref,
    tok, og, pin, pout, src, slot_of, gpt,
    mine_last, mine_rest, recv_last, recv_rest,
    held, ids, fixed_out, fixed_in, z_out, z_in,
    load_sem, xl_send, xl_recv, xr_send, xr_recv,
    id_send, id_recv, held_send, held_recv,
    fixed_send, fixed_recv, z_send, z_recv, token_a, token_b,
):
    j = lax.axis_index("dp")
    m = lax.axis_index("tensor")
    ndp = ny * nz * CORES
    half = ndp // 2
    core = lax.rem(j, CORES)
    z = lax.rem(lax.div(j, CORES), nz)
    y = lax.div(j, CORES * nz)

    def dp_of(yy, zz, cc):
        return (yy * nz + zz) * CORES + cc

    def rows_of(s):
        return pl.ds(s * length, length)

    last, rest = rows_of(3), pl.ds(0, 3 * length)
    loads = [
        (pout_hbm, pout),
        (og_hbm.at[last], og.at[last]),
        (pin_hbm, pin),
        (tok_hbm.at[last], tok.at[last]),
        (src_hbm, src),
        (slot_hbm, slot_of),
        (og_hbm.at[rest], og.at[rest]),
        (tok_hbm.at[rest], tok.at[rest]),
    ]
    loads = [pltpu.make_async_copy(a, b, load_sem.at[i]) for i, (a, b) in enumerate(loads)]
    for load in loads:
        load.start()

    def z_peers(offsets):
        offsets = sorted({d % nz for d in offsets} - {0})
        return [(dp_of(y, lax.rem(z + d, nz), core), m) for d in offsets]

    def greet(sem, peers):
        for peer in peers:
            pl.semaphore_signal(sem, inc=1, device_id=peer, device_id_type=MESH)

    x_peers = [(j, lax.rem(m + d, nx)) for d in range(1, nx)]
    spread = [(dy, dc) for dy in range(ny) for dc in range(CORES)]
    spread_peers = [
        (dp_of(lax.rem(y + dy, ny), z, lax.rem(core + dc, CORES)), m) for dy, dc in spread
    ]
    fixed_to = [lax.rem(j + ndp - 1, ndp), lax.rem(j + 1, ndp), lax.rem(j + half, ndp)]
    beside = lax.rem(j + ndp + 2 * core - 1, ndp)
    near = x_peers + spread_peers[1:] + z_peers((1, 2, -1, -2)) + [(beside, m)]
    two_off, four_off = z_peers((2, -2)), z_peers((4, -4))
    barrier = pltpu.get_barrier_semaphore()
    greet(barrier, near)

    def project(s, store):
        rows = rows_of(s)
        xp = product(tok[rows, :], pin[...])
        xp = jnp.concatenate([xp[: length // 2], xp[length // 2 :]], axis=1)
        gpt[s] = product(pout[...], og[rows, :])
        for q in range(nx):
            even = gpt[s, pl.ds(16 * q, 8, stride=2), :]
            odd = gpt[s, pl.ds(16 * q + 1, 8, stride=2), :]
            store(q, xp, jnp.concatenate([even, odd], axis=1))

    def store_last(q, xp, gq):
        mine_last[q, 0:32, :] = xp
        mine_last[q, 32:40, :] = gq

    for i in range(4):
        loads[i].wait()
    project(3, store_last)

    pl.semaphore_wait(barrier, len(near))
    for d in range(1, nx):
        pltpu.make_async_remote_copy(
            mine_last.at[x_peers[d - 1][1]], recv_last.at[nx - 1 - d], xl_send, xl_recv,
            device_id=x_peers[d - 1], device_id_type=MESH,
        ).start()
    greet(token_a, two_off)

    loads[4].wait()
    loads[5].wait()
    slots = [slot_of[src[i]] for i in range(4)]
    ids[0] = jnp.full((1, 128), slots[3], jnp.int32)

    def to_spread(source, target, send_sem, recv_sem):
        for t in range(1, len(spread)):
            dy, dc = spread[t]
            back = ((ny - dy) % ny) * CORES + dc
            pltpu.make_async_remote_copy(
                source.at[0], target.at[back], send_sem, recv_sem,
                device_id=spread_peers[t], device_id_type=MESH,
            ).start()

    to_spread(ids, ids, id_send, id_recv)

    loads[6].wait()
    loads[7].wait()
    for s in range(3):
        def store_rest(q, xp, gq):
            mine_rest[q, s, 0:32, :] = xp
            mine_rest[q, s, 32:40, :] = gq

        project(s, store_rest)
    for d in range(1, nx):
        pltpu.make_async_remote_copy(
            mine_rest.at[x_peers[d - 1][1]], recv_rest.at[nx - 1 - d], xr_send, xr_recv,
            device_id=x_peers[d - 1], device_id_type=MESH,
        ).start()

    pl.semaphore_wait(token_a, len(two_off))
    greet(token_b, four_off)

    low = lax.broadcasted_iota(jnp.int32, (32, 128), 1) < 64

    def sketch(total):
        xp, gq = total[0:32], total[32:40]
        turned = pltpu.roll(xp, 64, 1)
        twice = jnp.concatenate(
            [
                jnp.where(low, xp, 0.0), jnp.where(low, turned, 0.0),
                jnp.where(low, 0.0, turned), jnp.where(low, 0.0, xp),
            ],
            axis=0,
        )
        value = lax.dot_general(
            gq, twice, (((1,), (0,)), ((), ())),
            precision=lax.Precision.HIGHEST, preferred_element_type=F32,
        )
        return value * (length ** -0.5)

    pltpu.make_async_copy(recv_last, recv_last, xl_recv).wait()
    total = mine_last[m]
    for d in range(nx - 1):
        total = total + recv_last[d]
    held[0] = sketch(total)
    to_spread(held, held, held_send, held_recv)

    others = pl.ds(1, len(spread) - 1)
    pltpu.make_async_copy(ids.at[others], ids.at[others], id_recv).wait()
    if four_off:
        pl.semaphore_wait(token_b, len(four_off))
    pltpu.make_async_copy(held.at[others], held.at[others], held_recv).wait()

    def owner_rows(zz):
        base = dp_of(y, zz, core) * 2
        rows = []
        for w in range(2):
            acc = jnp.zeros((8, 128), F32)
            for i in range(len(spread)):
                acc = acc + jnp.where(ids[i] == base + w, held[i], 0.0)
            rows.append(acc)
        return rows

    for k in range(nz - 1):
        zz = k + lax.div(nz + k - z, nz)
        for w, row in enumerate(owner_rows(zz)):
            z_out[k, w] = row
        pltpu.make_async_remote_copy(
            z_out.at[k], z_in.at[lax.rem(z - zz + nz, nz)], z_send, z_recv,
            device_id=(dp_of(y, zz, core), m), device_id_type=MESH,
        ).start()
    for w, row in enumerate(owner_rows(z)):
        z_in[0, w] = row

    pltpu.make_async_copy(recv_rest, recv_rest, xr_recv).wait()
    for s in range(3):
        total = mine_rest[m, s]
        for d in range(nx - 1):
            total = total + recv_rest[d, s]
        value = sketch(total)
        for w in range(2):
            weight = jnp.where(slots[s] == fixed_to[s] * 2 + w, 1.0, 0.0).astype(F32)
            fixed_out[s, w] = value * weight
        pltpu.make_async_remote_copy(
            fixed_out.at[s], fixed_in.at[s], fixed_send.at[s], fixed_recv.at[s],
            device_id=(fixed_to[s], m), device_id_type=MESH,
        ).start()

    for s in range(3):
        pltpu.make_async_copy(fixed_in.at[s], fixed_in.at[s], fixed_recv.at[s]).wait()
    landed = z_in.at[pl.ds(1, nz - 1)]
    pltpu.make_async_copy(landed, landed, z_recv).wait()
    for w in range(2):
        acc = z_in[0, w]
        for s in range(3):
            acc = acc + fixed_in[s, w]
        for t in range(1, nz):
            acc = acc + z_in[t, w]
        out_ref[w] = acc

    pltpu.make_async_copy(recv_last, recv_last, xl_send).wait()
    pltpu.make_async_copy(recv_rest, recv_rest, xr_send).wait()
    pltpu.make_async_copy(ids.at[others], ids.at[others], id_send).wait()
    pltpu.make_async_copy(held.at[others], held.at[others], held_send).wait()
    for s in range(3):
        pltpu.make_async_copy(fixed_out.at[s], fixed_out.at[s], fixed_send.at[s]).wait()
    pltpu.make_async_copy(landed, landed, z_send).wait()


def local(ny, nz, nx, tokens, out_grad, proj_in, proj_out, source_ids, slot_of_source):
    length = tokens.shape[0] // source_ids.shape[0]
    pin, pout = proj_in.T, proj_out.T
    spread = ny * CORES
    dma, regular = pltpu.SemaphoreType.DMA, pltpu.SemaphoreType.REGULAR
    out = pl.pallas_call(
        functools.partial(kernel, ny, nz, nx, length),
        out_shape=jax.ShapeDtypeStruct((2, 8, 128), F32),
        in_specs=[pl.BlockSpec(memory_space=pl.ANY)] * 6,
        out_specs=pl.BlockSpec(memory_space=pltpu.VMEM),
        scratch_shapes=[
            pltpu.VMEM(tokens.shape, tokens.dtype),
            pltpu.VMEM(out_grad.shape, out_grad.dtype),
            pltpu.VMEM(pin.shape, pin.dtype),
            pltpu.VMEM(pout.shape, pout.dtype),
            pltpu.SMEM(source_ids.shape, jnp.int32),
            pltpu.SMEM(slot_of_source.shape, jnp.int32),
            pltpu.VMEM((4, 64, length), F32),
            pltpu.VMEM((nx, PACKED, 128), F32),
            pltpu.VMEM((nx, 3, PACKED, 128), F32),
            pltpu.VMEM((nx - 1, PACKED, 128), F32),
            pltpu.VMEM((nx - 1, 3, PACKED, 128), F32),
            pltpu.VMEM((spread, 8, 128), F32),
            pltpu.VMEM((spread, 1, 128), jnp.int32),
            pltpu.VMEM((3, 2, 8, 128), F32),
            pltpu.VMEM((3, 2, 8, 128), F32),
            pltpu.VMEM((nz, 2, 8, 128), F32),
            pltpu.VMEM((nz, 2, 8, 128), F32),
            dma((8,)), dma, dma, dma, dma, dma, dma, dma, dma, dma((3,)), dma((3,)), dma, dma,
            regular, regular,
        ],
        compiler_params=pltpu.CompilerParams(
            collective_id=0, has_side_effects=True, vmem_limit_bytes=60 * 2**20
        ),
    )(tokens, out_grad, pin, pout, source_ids, slot_of_source)
    return out.reshape(2, 8 * 128)


def solution(mesh):
    nx, ndp = mesh.shape["tensor"], mesh.shape["dp"]
    ny = COLUMNS
    nz = ndp // (ny * CORES)
    placed = (
        P("dp", "tensor"),
        P("dp", "tensor"),
        P("tensor", None),
        P("tensor", None),
        P("dp"),
        P(),
    )
    return jax.shard_map(
        functools.partial(local, ny, nz, nx),
        mesh=mesh, in_specs=placed, out_specs=P("dp", "tensor"), check_vma=False,
    )
```

time: 35.4 us -> 31.3 us (0.88); the launches traced: 35.2 us -> 30.8 us
  Pallas kernels: 33.9 us -> 29.5 us
    pallas_call x1, Pallas kernels: 33.9 us -> 29.5 us  [local(): pl.pallas_call(functools.partial(kernel, ny, nz, nx, length), out_shape=j...]
where the time goes in v2:
time: 31.3 us; the launch traced here: 30.8 us
  Pallas kernels  29.5 us (94%)
  local copies, waits for them, and re-layouts  1.3 us (4%)
    pallas_call x1, Pallas kernels, local(): pl.pallas_call(functools.partial(kernel, ny, nz, nx, length), out_shape=j...  29.5 us
    unnamed x1, local copies, waits for them, and re-layouts  1.3 us

profile of v2, /device:TPU:1, one launch (start us, length us, event | category | flops | bytes accessed | tf_op | source)
XLA Modules:
  0.0 30.8 jit_solution(6859008310319196618)
XLA Ops:
  0.0 29.5 %shard_map.64 = f32[2,8,128]{2,1,0:T(8,128)} custom-call(bf16[256,1024]{1,0:T(8,128)(2,1)} %tok_hbm.1, bf16[256,3584]{1,0:T(8,128)(2,1)} %og_hbm.1, bf16[64,1024]{1,0:T(8,128)(2,1)} %bitcast.7, bf16[64,3584]{1,0:T(8,128)(2,1)} %bitcast.6, s32[4]{0:T(128)} %src_hbm.1, s32[256]{0:T(256)} %slot_hbm.1), custom_call_target="tpu_custom_call" | custom-call | tf_op jit(solution)/shard_map/pallas_call | solution.py:232
  29.5 1.3 %copy.9 = f32[1,2,8,128]{3,1,2,0:T(2,128)} copy(f32[1,2,8,128]{3,2,1,0:T(8,128)} %bitcast.8) | data formatting | bytes 16384

commit v3 on v2

--- a/solution.py
+++ b/solution.py
@@ -12,6 +12,10 @@
 CORES = 2
 COLUMNS = 4
 PACKED = 40
+
+
+def away(d, n):
+    return min(d, n - d)
 
 
 def product(a, b):
@@ -71,6 +75,10 @@
     spread_peers = [
         (dp_of(lax.rem(y + dy, ny), z, lax.rem(core + dc, CORES)), m) for dy, dc in spread
     ]
+    x_order = sorted(range(1, nx), key=lambda d: -away(d, nx))
+    spread_order = sorted(
+        range(1, len(spread)), key=lambda t: (-away(spread[t][0], ny), -spread[t][1])
+    )
     fixed_to = [lax.rem(j + ndp - 1, ndp), lax.rem(j + 1, ndp), lax.rem(j + half, ndp)]
     beside = lax.rem(j + ndp + 2 * core - 1, ndp)
     near = x_peers + spread_peers[1:] + z_peers((1, 2, -1, -2)) + [(beside, m)]
@@ -97,7 +105,7 @@
     project(3, store_last)
 
     pl.semaphore_wait(barrier, len(near))
-    for d in range(1, nx):
+    for d in x_order:
         pltpu.make_async_remote_copy(
             mine_last.at[x_peers[d - 1][1]], recv_last.at[nx - 1 - d], xl_send, xl_recv,
             device_id=x_peers[d - 1], device_id_type=MESH,
@@ -110,7 +118,7 @@
     ids[0] = jnp.full((1, 128), slots[3], jnp.int32)
 
     def to_spread(source, target, send_sem, recv_sem):
-        for t in range(1, len(spread)):
+        for t in spread_order:
             dy, dc = spread[t]
             back = ((ny - dy) % ny) * CORES + dc
             pltpu.make_async_remote_copy(
@@ -128,14 +136,14 @@
             mine_rest[q, s, 32:40, :] = gq
 
         project(s, store_rest)
-    for d in range(1, nx):
+    pl.semaphore_wait(token_a, len(two_off))
+    greet(token_b, four_off)
+
+    for d in x_order:
         pltpu.make_async_remote_copy(
             mine_rest.at[x_peers[d - 1][1]], recv_rest.at[nx - 1 - d], xr_send, xr_recv,
             device_id=x_peers[d - 1], device_id_type=MESH,
         ).start()
-
-    pl.semaphore_wait(token_a, len(two_off))
-    greet(token_b, four_off)
 
     low = lax.broadcasted_iota(jnp.int32, (32, 128), 1) < 64
 
@@ -231,7 +239,7 @@
     dma, regular = pltpu.SemaphoreType.DMA, pltpu.SemaphoreType.REGULAR
     out = pl.pallas_call(
         functools.partial(kernel, ny, nz, nx, length),
-        out_shape=jax.ShapeDtypeStruct((2, 8, 128), F32),
+        out_shape=pltpu.VMEM((2, 8, 128), F32),
         in_specs=[pl.BlockSpec(memory_space=pl.ANY)] * 6,
         out_specs=pl.BlockSpec(memory_space=pltpu.VMEM),
         scratch_shapes=[

time: 31.3 us -> 29.3 us (0.936)
  the two profiles are of different devices: /device:TPU:1 before, /device:TPU:32 now
where the time goes in v3:
time: 29.3 us; the launch traced here: 29.2 us
  Pallas kernels  28.5 us (97%)
  local copies, waits for them, and re-layouts  0.6 us (2%)
    pallas_call x1, Pallas kernels, local(): pl.pallas_call(functools.partial(kernel, ny, nz, nx, length), out_shape=p...  28.5 us
    unnamed x1, local copies, waits for them, and re-layouts  0.6 us

profile of v3, /device:TPU:32, one launch (start us, length us, event | category | flops | bytes accessed | tf_op | source)
XLA Modules:
  0.0 29.2 jit_solution(10915037622895874435)
XLA Ops:
  0.0 28.5 %shard_map.64 = f32[2,8,128]{2,1,0:T(8,128)S(1)} custom-call(bf16[256,1024]{1,0:T(8,128)(2,1)} %tok_hbm.1, bf16[256,3584]{1,0:T(8,128)(2,1)} %og_hbm.1, bf16[64,1024]{1,0:T(8,128)(2,1)} %bitcast.8, bf16[64,3584]{1,0:T(8,128)(2,1)} %bitcast.7, s32[4]{0:T(128)} %src_hbm.1, s32[256]{0:T(256)} %slot_hbm.1), custom_call_target="tpu_custom_call" | custom-call | tf_op jit(solution)/shard_map/pallas_call | solution.py:240
  28.6 0.6 %copy.9 = f32[1,2,8,128]{3,1,2,0:T(2,128)} copy(f32[1,2,8,128]{3,2,1,0:T(8,128)S(1)} %bitcast.6) | data formatting | bytes 16384

commit v4 on v3

--- a/solution.py
+++ b/solution.py
@@ -11,6 +11,8 @@
 F32 = jnp.float32
 CORES = 2
 COLUMNS = 4
+HEADS = 5
+FIRST = ((0, 1),)
 PACKED = 40
 
 
@@ -28,10 +30,11 @@
     out_ref,
     tok, og, pin, pout, src, slot_of, gpt,
     mine_last, mine_rest, recv_last, recv_rest,
-    held, ids, fixed_out, fixed_in, z_out, z_in,
+    held, ids, fixed_out, fixed_in, y_out, y_in,
+    straight, straight_ids, straight_send, straight_recv, straight_id_send, straight_id_recv,
     load_sem, xl_send, xl_recv, xr_send, xr_recv,
     id_send, id_recv, held_send, held_recv,
-    fixed_send, fixed_recv, z_send, z_recv, token_a, token_b,
+    fixed_send, fixed_recv, y_send, y_recv, token_a, token_b,
 ):
     j = lax.axis_index("dp")
     m = lax.axis_index("tensor")
@@ -85,6 +88,30 @@
     two_off, four_off = z_peers((2, -2)), z_peers((4, -4))
     barrier = pltpu.get_barrier_semaphore()
     greet(barrier, near)
+    heads = HEADS if nz >= 16 else 0
+
+    @pl.when(z < heads)
+    def _():
+        greet(barrier, z_peers(range(1, nz)))
+
+    far = range(nz // 2 - 1, nz // 2 + 4) if heads else range(0)
+    firsts = FIRST if heads else ()
+    is_far = jnp.logical_and(z >= nz // 2 - 1, z <= nz // 2 + 3)
+    far_group = lax.div(z + nz // 2 + 1, nz) - lax.div(z + nz // 2 - 4, nz)
+
+    def at_first(yy, cc):
+        at = z < 0
+        for fy, fc in firsts:
+            at = jnp.logical_or(at, jnp.logical_and(yy == fy, cc == fc))
+        return at
+
+    is_first = jnp.logical_and(z == 0, at_first(y, core))
+
+    @pl.when(is_first)
+    def _():
+        for zz in far:
+            greet(barrier, [(dp_of(yy, zz, cc), m) for yy in range(ny) for cc in range(CORES)])
+
 
     def project(s, store):
         rows = rows_of(s)
@@ -104,7 +131,19 @@
         loads[i].wait()
     project(3, store_last)
 
-    pl.semaphore_wait(barrier, len(near))
+    @pl.when(z < heads)
+    def _():
+        pl.semaphore_wait(barrier, len(near) + heads - 1)
+
+    @pl.when(jnp.logical_and(z >= heads, jnp.logical_not(is_far)))
+    def _():
+        pl.semaphore_wait(barrier, len(near) + heads)
+
+    if heads:
+        @pl.when(is_far)
+        def _():
+            pl.semaphore_wait(barrier, len(near) + heads + len(firsts))
+
     for d in x_order:
         pltpu.make_async_remote_copy(
             mine_last.at[x_peers[d - 1][1]], recv_last.at[nx - 1 - d], xl_send, xl_recv,
@@ -117,16 +156,30 @@
     slots = [slot_of[src[i]] for i in range(4)]
     ids[0] = jnp.full((1, 128), slots[3], jnp.int32)
 
-    def to_spread(source, target, send_sem, recv_sem):
-        for t in spread_order:
-            dy, dc = spread[t]
-            back = ((ny - dy) % ny) * CORES + dc
-            pltpu.make_async_remote_copy(
-                source.at[0], target.at[back], send_sem, recv_sem,
-                device_id=spread_peers[t], device_id_type=MESH,
-            ).start()
-
-    to_spread(ids, ids, id_send, id_recv)
+    def along_z(source, targets, send_sem, recv_sem):
+        for zz in targets:
+            @pl.when(z != zz)
+            def _():
+                pltpu.make_async_remote_copy(
+                    source.at[0], source.at[lax.rem(z - zz + nz, nz)], send_sem, recv_sem,
+                    device_id=(dp_of(y, zz, core), m), device_id_type=MESH,
+                ).start()
+
+    def to_first(source, target, send_sem, recv_sem):
+        if not firsts:
+            return
+
+        @pl.when(is_far)
+        def _():
+            for fy, fc in firsts:
+                pltpu.make_async_remote_copy(
+                    source.at[0], target.at[z - far[0], y * CORES + core], send_sem, recv_sem,
+                    device_id=(dp_of(fy, 0, fc), m), device_id_type=MESH,
+                ).start()
+
+    early, late = range(heads), range(heads, nz)
+    to_first(ids, straight_ids, straight_id_send, straight_id_recv)
+    along_z(ids, early, id_send, id_recv)
 
     loads[6].wait()
     loads[7].wait()
@@ -168,34 +221,12 @@
     for d in range(nx - 1):
         total = total + recv_last[d]
     held[0] = sketch(total)
-    to_spread(held, held, held_send, held_recv)
-
-    others = pl.ds(1, len(spread) - 1)
-    pltpu.make_async_copy(ids.at[others], ids.at[others], id_recv).wait()
+    to_first(held, straight, straight_send, straight_recv)
+    along_z(held, early, held_send, held_recv.at[far_group])
     if four_off:
         pl.semaphore_wait(token_b, len(four_off))
-    pltpu.make_async_copy(held.at[others], held.at[others], held_recv).wait()
-
-    def owner_rows(zz):
-        base = dp_of(y, zz, core) * 2
-        rows = []
-        for w in range(2):
-            acc = jnp.zeros((8, 128), F32)
-            for i in range(len(spread)):
-                acc = acc + jnp.where(ids[i] == base + w, held[i], 0.0)
-            rows.append(acc)
-        return rows
-
-    for k in range(nz - 1):
-        zz = k + lax.div(nz + k - z, nz)
-        for w, row in enumerate(owner_rows(zz)):
-            z_out[k, w] = row
-        pltpu.make_async_remote_copy(
-            z_out.at[k], z_in.at[lax.rem(z - zz + nz, nz)], z_send, z_recv,
-            device_id=(dp_of(y, zz, core), m), device_id_type=MESH,
-        ).start()
-    for w, row in enumerate(owner_rows(z)):
-        z_in[0, w] = row
+    along_z(ids, late, id_send, id_recv)
+    along_z(held, late, held_send, held_recv.at[far_group])
 
     pltpu.make_async_copy(recv_rest, recv_rest, xr_recv).wait()
     for s in range(3):
@@ -211,17 +242,99 @@
             device_id=(fixed_to[s], m), device_id_type=MESH,
         ).start()
 
+    others = pl.ds(1, nz - 1)
+    pltpu.make_async_copy(ids.at[others], ids.at[others], id_recv).wait()
+
+    def arrived(count, group):
+        slots = held.at[pl.ds(0, count)]
+        pltpu.make_async_copy(slots, slots, held_recv.at[group]).wait()
+
+    def add(t, slots, fresh):
+        base = spread_peers[t][0] * 2
+        for w in range(2):
+            acc = jnp.zeros((8, 128), F32) if fresh else y_out[t, w]
+            for i in slots:
+                acc = acc + jnp.where(ids[i] == base + w, held[i], 0.0)
+            y_out[t, w] = acc
+
+    def to_spread(t):
+        if t:
+            dy, dc = spread[t]
+            back = ((ny - dy) % ny) * CORES + dc
+            pltpu.make_async_remote_copy(
+                y_out.at[t], y_in.at[back], y_send, y_recv,
+                device_id=spread_peers[t], device_id_type=MESH,
+            ).start()
+
+    def goes_first(t):
+        dy, dc = spread[t]
+        return at_first(lax.rem(y + dy, ny), lax.rem(core + dc, CORES))
+
+    if heads:
+        @pl.when(z == 0)
+        def _():
+            arrived(nz - 1 - len(far), 0)
+            for t in spread_order + [0]:
+                add(t, [i for i in range(nz) if i not in far], True)
+
+                @pl.when(goes_first(t))
+                def _():
+                    to_spread(t)
+
+            arrived(len(far), 1)
+            for t in spread_order + [0]:
+                @pl.when(jnp.logical_not(goes_first(t)))
+                def _():
+                    add(t, far, False)
+                    to_spread(t)
+
+    @pl.when(z >= (1 if heads else 0))
+    def _():
+        if heads:
+            @pl.when(is_far)
+            def _():
+                arrived(nz - len(far), 0)
+                arrived(len(far) - 1, 1)
+
+            @pl.when(jnp.logical_not(is_far))
+            def _():
+                arrived(nz - 1 - len(far), 0)
+                arrived(len(far), 1)
+        else:
+            arrived(nz - 1, 0)
+        for t in spread_order + [0]:
+            add(t, range(nz), True)
+            to_spread(t)
+
     for s in range(3):
         pltpu.make_async_copy(fixed_in.at[s], fixed_in.at[s], fixed_recv.at[s]).wait()
-    landed = z_in.at[pl.ds(1, nz - 1)]
-    pltpu.make_async_copy(landed, landed, z_recv).wait()
+    landed = y_in.at[pl.ds(1, len(spread) - 1)]
+    pltpu.make_async_copy(landed, landed, y_recv).wait()
     for w in range(2):
-        acc = z_in[0, w]
+        acc = y_out[0, w]
         for s in range(3):
             acc = acc + fixed_in[s, w]
-        for t in range(1, nz):
-            acc = acc + z_in[t, w]
+        for t in range(1, len(spread)):
+            acc = acc + y_in[t, w]
         out_ref[w] = acc
+
+    if firsts:
+        @pl.when(is_first)
+        def _():
+            for buffer, sem in ((straight_ids, straight_id_recv), (straight, straight_recv)):
+                pltpu.make_async_copy(buffer, buffer, sem).wait()
+            for w in range(2):
+                acc = out_ref[w]
+                for i in range(len(far)):
+                    for t in range(len(spread)):
+                        acc = acc + jnp.where(straight_ids[i, t] == j * 2 + w, straight[i, t], 0.0)
+                out_ref[w] = acc
+
+        @pl.when(is_far)
+        def _():
+            for buffer, sem in ((straight_ids, straight_id_send), (straight, straight_send)):
+                sent = buffer.at[0, pl.ds(0, len(firsts))]
+                pltpu.make_async_copy(sent, sent, sem).wait()
 
     pltpu.make_async_copy(recv_last, recv_last, xl_send).wait()
     pltpu.make_async_copy(recv_rest, recv_rest, xr_send).wait()
@@ -229,7 +342,7 @@
     pltpu.make_async_copy(held.at[others], held.at[others], held_send).wait()
     for s in range(3):
         pltpu.make_async_copy(fixed_out.at[s], fixed_out.at[s], fixed_send.at[s]).wait()
-    pltpu.make_async_copy(landed, landed, z_send).wait()
+    pltpu.make_async_copy(landed, landed, y_send).wait()
 
 
 def local(ny, nz, nx, tokens, out_grad, proj_in, proj_out, source_ids, slot_of_source):
@@ -254,13 +367,16 @@
             pltpu.VMEM((nx, 3, PACKED, 128), F32),
             pltpu.VMEM((nx - 1, PACKED, 128), F32),
             pltpu.VMEM((nx - 1, 3, PACKED, 128), F32),
-            pltpu.VMEM((spread, 8, 128), F32),
-            pltpu.VMEM((spread, 1, 128), jnp.int32),
+            pltpu.VMEM((nz, 8, 128), F32),
+            pltpu.VMEM((nz, 1, 128), jnp.int32),
             pltpu.VMEM((3, 2, 8, 128), F32),
             pltpu.VMEM((3, 2, 8, 128), F32),
-            pltpu.VMEM((nz, 2, 8, 128), F32),
-            pltpu.VMEM((nz, 2, 8, 128), F32),
-            dma((8,)), dma, dma, dma, dma, dma, dma, dma, dma, dma((3,)), dma((3,)), dma, dma,
+            pltpu.VMEM((spread, 2, 8, 128), F32),
+            pltpu.VMEM((spread, 2, 8, 128), F32),
+            pltpu.VMEM((5, spread, 8, 128), F32),
+            pltpu.VMEM((5, spread, 1, 128), jnp.int32),
+            dma, dma, dma, dma,
+            dma((8,)), dma, dma, dma, dma, dma, dma, dma, dma((2,)), dma((3,)), dma((3,)), dma, dma,
             regular, regular,
         ],
         compiler_params=pltpu.CompilerParams(

time: 29.3 us -> 28.7 us (0.980)
  the two profiles are of different devices: /device:TPU:32 before, /device:TPU:1 now
where the time goes in v4:
time: 28.7 us; the launch traced here: 28.5 us
  Pallas kernels  27.9 us (97%)
  local copies, waits for them, and re-layouts  0.6 us (2%)
    pallas_call x1, Pallas kernels, local(): pl.pallas_call(functools.partial(kernel, ny, nz, nx, length), out_shape=p...  27.9 us
    unnamed x1, local copies, waits for them, and re-layouts  0.6 us

profile of v4, /device:TPU:1, one launch (start us, length us, event | category | flops | bytes accessed | tf_op | source)
XLA Modules:
  0.0 28.5 jit_solution(3217119785950760316)
XLA Ops:
  0.0 27.9 %shard_map.64 = f32[2,8,128]{2,1,0:T(8,128)S(1)} custom-call(bf16[256,1024]{1,0:T(8,128)(2,1)} %tok_hbm.1, bf16[256,3584]{1,0:T(8,128)(2,1)} %og_hbm.1, bf16[64,1024]{1,0:T(8,128)(2,1)} %bitcast.8, bf16[64,3584]{1,0:T(8,128)(2,1)} %bitcast.7, s32[4]{0:T(128)} %src_hbm.1, s32[256]{0:T(256)} %slot_hbm.1), custom_call_target="tpu_custom_call" | custom-call | tf_op jit(solution)/shard_map/pallas_call | solution.py:353
  27.9 0.6 %copy.9 = f32[1,2,8,128]{3,1,2,0:T(2,128)} copy(f32[1,2,8,128]{3,2,1,0:T(8,128)S(1)} %bitcast.6) | data formatting | bytes 16384

commit v5 on v4

--- a/solution.py
+++ b/solution.py
@@ -13,6 +13,7 @@
 COLUMNS = 4
 HEADS = 5
 FIRST = ((0, 1),)
+FAR = 7
 PACKED = 40
 
 
@@ -94,10 +95,11 @@
     def _():
         greet(barrier, z_peers(range(1, nz)))
 
-    far = range(nz // 2 - 1, nz // 2 + 4) if heads else range(0)
+    begin, end = nz // 2 - FAR // 2 + 1, nz // 2 + FAR // 2 + 2
+    far = range(begin, end) if heads else range(0)
     firsts = FIRST if heads else ()
-    is_far = jnp.logical_and(z >= nz // 2 - 1, z <= nz // 2 + 3)
-    far_group = lax.div(z + nz // 2 + 1, nz) - lax.div(z + nz // 2 - 4, nz)
+    is_far = jnp.logical_and(z >= begin, z < end)
+    far_group = lax.div(z + nz - begin, nz) - lax.div(z + nz - end, nz)
 
     def at_first(yy, cc):
         at = z < 0
@@ -221,8 +223,9 @@
     for d in range(nx - 1):
         total = total + recv_last[d]
     held[0] = sketch(total)
+    along_z(held, range(1), held_send, held_recv.at[far_group])
     to_first(held, straight, straight_send, straight_recv)
-    along_z(held, early, held_send, held_recv.at[far_group])
+    along_z(held, range(1, heads), held_send, held_recv.at[far_group])
     if four_off:
         pl.semaphore_wait(token_b, len(four_off))
     along_z(ids, late, id_send, id_recv)
@@ -373,8 +376,8 @@
             pltpu.VMEM((3, 2, 8, 128), F32),
             pltpu.VMEM((spread, 2, 8, 128), F32),
             pltpu.VMEM((spread, 2, 8, 128), F32),
-            pltpu.VMEM((5, spread, 8, 128), F32),
-            pltpu.VMEM((5, spread, 1, 128), jnp.int32),
+            pltpu.VMEM((FAR, spread, 8, 128), F32),
+            pltpu.VMEM((FAR, spread, 1, 128), jnp.int32),
             dma, dma, dma, dma,
             dma((8,)), dma, dma, dma, dma, dma, dma, dma, dma((2,)), dma((3,)), dma((3,)), dma, dma,
             regular, regular,

time: 28.7 us -> 28.2 us (0.983)
  the two profiles are of different devices: /device:TPU:1 before, /device:TPU:2 now
where the time goes in v5:
time: 28.2 us; the launch traced here: 28.1 us
  Pallas kernels  27.5 us (98%)
  local copies, waits for them, and re-layouts  0.6 us (2%)
    pallas_call x1, Pallas kernels, local(): pl.pallas_call(functools.partial(kernel, ny, nz, nx, length), out_shape=p...  27.5 us
    unnamed x1, local copies, waits for them, and re-layouts  0.6 us

profile of v5, /device:TPU:2, one launch (start us, length us, event | category | flops | bytes accessed | tf_op | source)
XLA Modules:
  0.0 28.1 jit_solution(9626924926527791757)
XLA Ops:
  0.0 27.5 %shard_map.64 = f32[2,8,128]{2,1,0:T(8,128)S(1)} custom-call(bf16[256,1024]{1,0:T(8,128)(2,1)} %tok_hbm.1, bf16[256,3584]{1,0:T(8,128)(2,1)} %og_hbm.1, bf16[64,1024]{1,0:T(8,128)(2,1)} %bitcast.8, bf16[64,3584]{1,0:T(8,128)(2,1)} %bitcast.7, s32[4]{0:T(128)} %src_hbm.1, s32[256]{0:T(256)} %slot_hbm.1), custom_call_target="tpu_custom_call" | custom-call | tf_op jit(solution)/shard_map/pallas_call | solution.py:356
  27.5 0.6 %copy.9 = f32[1,2,8,128]{3,1,2,0:T(2,128)} copy(f32[1,2,8,128]{3,2,1,0:T(8,128)S(1)} %bitcast.6) | data formatting | bytes 16384

commit v6 on v5

--- a/solution.py
+++ b/solution.py
@@ -11,7 +11,7 @@
 F32 = jnp.float32
 CORES = 2
 COLUMNS = 4
-HEADS = 5
+HEADS = 4
 FIRST = ((0, 1),)
 FAR = 7
 PACKED = 40
@@ -119,7 +119,7 @@
         rows = rows_of(s)
         xp = product(tok[rows, :], pin[...])
         xp = jnp.concatenate([xp[: length // 2], xp[length // 2 :]], axis=1)
-        gpt[s] = product(pout[...], og[rows, :])
+        gpt[s, 0:64, :] = product(pout[...], og[rows, :])
         for q in range(nx):
             even = gpt[s, pl.ds(16 * q, 8, stride=2), :]
             odd = gpt[s, pl.ds(16 * q + 1, 8, stride=2), :]
@@ -183,6 +183,9 @@
     to_first(ids, straight_ids, straight_id_send, straight_id_recv)
     along_z(ids, early, id_send, id_recv)
 
+    pl.semaphore_wait(token_a, len(two_off))
+    greet(token_b, four_off)
+
     loads[6].wait()
     loads[7].wait()
     for s in range(3):
@@ -191,14 +194,6 @@
             mine_rest[q, s, 32:40, :] = gq
 
         project(s, store_rest)
-    pl.semaphore_wait(token_a, len(two_off))
-    greet(token_b, four_off)
-
-    for d in x_order:
-        pltpu.make_async_remote_copy(
-            mine_rest.at[x_peers[d - 1][1]], recv_rest.at[nx - 1 - d], xr_send, xr_recv,
-            device_id=x_peers[d - 1], device_id_type=MESH,
-        ).start()
 
     low = lax.broadcasted_iota(jnp.int32, (32, 128), 1) < 64
 
@@ -226,6 +221,12 @@
     along_z(held, range(1), held_send, held_recv.at[far_group])
     to_first(held, straight, straight_send, straight_recv)
     along_z(held, range(1, heads), held_send, held_recv.at[far_group])
+    for d in x_order:
+        pltpu.make_async_remote_copy(
+            mine_rest.at[x_peers[d - 1][1]], recv_rest.at[nx - 1 - d], xr_send, xr_recv,
+            device_id=x_peers[d - 1], device_id_type=MESH,
+        ).start()
+
     if four_off:
         pl.semaphore_wait(token_b, len(four_off))
     along_z(ids, late, id_send, id_recv)
@@ -365,7 +366,7 @@
             pltpu.VMEM(pout.shape, pout.dtype),
             pltpu.SMEM(source_ids.shape, jnp.int32),
             pltpu.SMEM(slot_of_source.shape, jnp.int32),
-            pltpu.VMEM((4, 64, length), F32),
+            pltpu.VMEM((4, 72, length), F32),
             pltpu.VMEM((nx, PACKED, 128), F32),
             pltpu.VMEM((nx, 3, PACKED, 128), F32),
             pltpu.VMEM((nx - 1, PACKED, 128), F32),

time: 28.2 us -> 28.2 us (level)
  the two profiles are of different devices: /device:TPU:2 before, /device:TPU:1 now
where the time goes in v6:
time: 28.2 us; the launch traced here: 27.7 us
  Pallas kernels  27.1 us (96%)
  local copies, waits for them, and re-layouts  0.6 us (2%)
    pallas_call x1, Pallas kernels, local(): pl.pallas_call(functools.partial(kernel, ny, nz, nx, length), out_shape=p...  27.1 us
    unnamed x1, local copies, waits for them, and re-layouts  0.6 us

profile of v6, /device:TPU:1, one launch (start us, length us, event | category | flops | bytes accessed | tf_op | source)
XLA Modules:
  0.0 27.7 jit_solution(15388536470101391332)
XLA Ops:
  0.0 27.1 %shard_map.64 = f32[2,8,128]{2,1,0:T(8,128)S(1)} custom-call(bf16[256,1024]{1,0:T(8,128)(2,1)} %tok_hbm.1, bf16[256,3584]{1,0:T(8,128)(2,1)} %og_hbm.1, bf16[64,1024]{1,0:T(8,128)(2,1)} %bitcast.8, bf16[64,3584]{1,0:T(8,128)(2,1)} %bitcast.7, s32[4]{0:T(128)} %src_hbm.1, s32[256]{0:T(256)} %slot_hbm.1), custom_call_target="tpu_custom_call" | custom-call | tf_op jit(solution)/shard_map/pallas_call | solution.py:357
  27.1 0.6 %copy.9 = f32[1,2,8,128]{3,1,2,0:T(2,128)} copy(f32[1,2,8,128]{3,2,1,0:T(8,128)S(1)} %bitcast.6) | data formatting | bytes 16384

commit v7 on v6

--- a/solution.py
+++ b/solution.py
@@ -12,7 +12,7 @@
 CORES = 2
 COLUMNS = 4
 HEADS = 4
-FIRST = ((0, 1),)
+FIRST = ((0, 1), (1, 1))
 FAR = 7
 PACKED = 40
 

time: 28.2 us -> 28 us (level)
  no operation moved by 1% of the time
where the time goes in v7:
time: 28 us; the launch traced here: 27.7 us
  Pallas kernels  27.1 us (97%)
  local copies, waits for them, and re-layouts  0.6 us (2%)
    pallas_call x1, Pallas kernels, local(): pl.pallas_call(functools.partial(kernel, ny, nz, nx, length), out_shape=p...  27.1 us
    unnamed x1, local copies, waits for them, and re-layouts  0.6 us

profile of v7, /device:TPU:1, one launch (start us, length us, event | category | flops | bytes accessed | tf_op | source)
XLA Modules:
  0.0 27.7 jit_solution(6621590305848472255)
XLA Ops:
  0.0 27.1 %shard_map.64 = f32[2,8,128]{2,1,0:T(8,128)S(1)} custom-call(bf16[256,1024]{1,0:T(8,128)(2,1)} %tok_hbm.1, bf16[256,3584]{1,0:T(8,128)(2,1)} %og_hbm.1, bf16[64,1024]{1,0:T(8,128)(2,1)} %bitcast.8, bf16[64,3584]{1,0:T(8,128)(2,1)} %bitcast.7, s32[4]{0:T(128)} %src_hbm.1, s32[256]{0:T(256)} %slot_hbm.1), custom_call_target="tpu_custom_call" | custom-call | tf_op jit(solution)/shard_map/pallas_call | solution.py:357
  27.1 0.6 %copy.9 = f32[1,2,8,128]{3,1,2,0:T(2,128)} copy(f32[1,2,8,128]{3,2,1,0:T(8,128)S(1)} %bitcast.6) | data formatting | bytes 16384
